TPU v7x, 32 devices: a whole 2x2x4 slice. The times are simulated.
32 devices in a mesh: pipe: 4 (over y, x), ctx: 8 (over z, core).
Axes of the slice: x: 2, y: 2, z: 4, core: 2. Of those that a mesh axis runs over, the one named last changes fastest.
Arguments:
- x_in: bfloat16 [4, 512, 8192], P('pipe', 'ctx'), may hold values from -6 to 6
- z_in: bfloat16 [4, 512, 8192], P('pipe', 'ctx'), may hold values from -6 to 6
- bc_in: bfloat16 [4, 512, 1024], P('pipe', 'ctx'), may hold values from -6 to 6
- dt_raw: bfloat16 [4, 512, 128], P('pipe', 'ctx'), may hold values from -3.2 to 3.2
- a_log: float32 [4, 128], P('pipe'), may hold values from -12 to 3
- dt_bias: float32 [4, 128], P('pipe'), may hold values from -3.8 to -3
- d_skip: float32 [4, 128], P('pipe'), may hold values from 0.5 to 1.5
- conv_x: bfloat16 [4, 4, 8192], P('pipe'), may hold values from -3 to 3
- conv_bc: bfloat16 [4, 4, 1024], P('pipe'), may hold values from -3 to 3
- norm_gain: float32 [4, 8192], P('pipe'), may hold values from 0.5 to 1.5
- seg_ids: int32 [4, 512], P('pipe', 'ctx'), may hold values from 0 to 3, never falling along the last dimension, each value on 1 to 256 neighbouring positions
- query: bfloat16 [4, 512, 2048], P('pipe', 'ctx'), may hold values from -192 to 192
- keys: bfloat16 [4, 512, 256], P('pipe', 'ctx'), may hold values from -6 to 6
- values: bfloat16 [4, 512, 256], P('pipe', 'ctx'), may hold values from -6 to 6
Outputs:
- mamba_out: bfloat16 [4, 512, 8192], P('pipe', 'ctx')
- handoff: bfloat16 [4, 512, 2048], P('pipe', 'ctx')
Inputs may be any that keep to these rules, and one draw needn't show every extreme that they name: `seg_ids`: segment numbers never fall along a section's sequence; no segment is longer than 256 positions, and one has exactly that many.
All inputs are finite; a program needn't handle non-finite values.
Results may differ from a plain program's by a relative error of at most 0.0044.
The roundings to bfloat16 on the way count: a program that leaves them out, or rounds other values in their place, can miss the bound.
Values may be sent and summed in bfloat16 or wider, within the bound.
No kernel may reach another device: no remote copies, remote signals or barrier semaphores. Data moves between devices by JAX's collectives and lax.ppermute only.
A program may use at most 128 MiB of HBM per device.

v0:
```python
import math
import jax
import jax.numpy as jnp
from jax import lax
from jax.sharding import PartitionSpec as P

G = 4
AH = 32
KVH = 4
HD = 64
norm_eps = 1e-05


def from_behind(value, axis, steps):
    count = lax.axis_size(axis)
    pairs = [(source, (source + steps) % count) for source in range(count)]
    return lax.ppermute(value, axis, pairs)


def causal_taps(rim, inputs, rim_ids, ids, weights):
    lag = rim.shape[0]
    length = inputs.shape[0]
    padded = jnp.concatenate([rim, inputs], axis=0)
    padded_ids = jnp.concatenate([rim_ids, ids])
    layout = (length,) + (1,) * (inputs.ndim - 1)
    summed = jnp.zeros(inputs.shape, jnp.float32)
    for tap in range(lag + 1):
        same = (padded_ids[tap : tap + length] == ids).reshape(layout)
        summed = summed + jnp.where(
            same,
            weights[tap].astype(jnp.float32) * padded[tap : tap + length].astype(jnp.float32),
            0.0,
        )
    return jax.nn.silu(summed).astype(jnp.bfloat16)


def per_head(grouped, heads):
    leading = grouped.shape[:-3]
    groups = grouped.shape[-2]
    states = grouped.shape[-1]
    moved = jnp.swapaxes(grouped, -3, -2)
    spread = jnp.repeat(moved, heads // groups, axis=-3)
    return spread.reshape(leading + (heads, 2 * states))


def state_space(x_conv, bc_conv, step_size, rates, skip, ids):
    length, local_heads, head_dim = x_conv.shape
    states = bc_conv.shape[2] // 2
    span = min(256, length)
    blocks = length // span
    lower = jnp.arange(span)[:, None] >= jnp.arange(span)[None, :]

    def advance(carry, item):
        memory, last_id = carry
        x_block, bc_block, step_block, id_block = item
        b_part = bc_block[:, :, :states]
        c_part = bc_block[:, :, states:]
        logs = jnp.cumsum(step_block * rates[None, :], axis=0)
        allowed = lower & (id_block[:, None] == id_block[None, :])
        gaps = logs[:, None, :] - logs[None, :, :]
        weights = (
            jnp.where(allowed[:, :, None], jnp.exp(jnp.minimum(gaps, 0.0)), 0.0)
            * step_block[None, :, :]
        )
        inner = jnp.einsum("thn,shn->tsh", c_part, b_part, preferred_element_type=jnp.float32)
        mixing = (inner * weights).astype(jnp.bfloat16)
        local_part = jnp.einsum("tsh,shp->thp", mixing, x_block, preferred_element_type=jnp.float32)
        keep = jnp.where((id_block == last_id)[:, None], jnp.exp(logs), 0.0)
        carried = (
            jnp.einsum(
                "thn,hpn->thp", c_part.astype(jnp.float32), memory, precision=lax.Precision.HIGHEST
            )
            * keep[:, :, None]
        )
        result = local_part + carried + skip[None, :, None] * x_block.astype(jnp.float32)
        tail = logs[span - 1]
        writes = (
            jnp.where((id_block == id_block[span - 1])[:, None], jnp.exp(tail[None, :] - logs), 0.0)
            * step_block
        )
        scaled = (x_block.astype(jnp.float32) * writes[:, :, None]).astype(jnp.bfloat16)
        added = jnp.einsum("shp,shn->hpn", scaled, b_part, preferred_element_type=jnp.float32)
        kept = jnp.where(id_block[span - 1] == last_id, jnp.exp(tail), 0.0)
        memory = memory * kept[:, None, None] + added
        return ((memory, id_block[span - 1]), result)

    start = (jnp.zeros((local_heads, head_dim, states), jnp.float32), jnp.array(-1, jnp.int32))
    items = (
        x_conv.reshape(blocks, span, local_heads, head_dim),
        bc_conv.reshape(blocks, span, local_heads, 2 * states),
        step_size.reshape(blocks, span, local_heads),
        ids.reshape(blocks, span),
    )
    (memory, _), outputs = lax.scan(advance, start, items)
    return (memory, outputs.reshape(length, local_heads, head_dim))


def on_device(
    x_in,
    z_in,
    bc_in,
    dt_raw,
    a_log,
    dt_bias,
    d_skip,
    conv_x,
    conv_bc,
    norm_gain,
    seg_ids,
    query,
    keys,
    values,
):
    ranks = lax.axis_size("ctx")
    place = lax.axis_index("ctx")
    tokens_here = x_in.shape[1]
    heads = dt_raw.shape[2]
    head_dim = x_in.shape[2] // heads
    states = bc_in.shape[2] // (2 * G)
    lag = conv_x.shape[1] - 1
    own_ids = seg_ids[0]
    all_ids = lax.all_gather(own_ids, "ctx", axis=0, tiled=True)
    local_heads = heads // ranks
    first_head = place * local_heads
    x_send = x_in[0].reshape(tokens_here, heads, head_dim)
    bc_send = per_head(bc_in[0].reshape(tokens_here, 2, G, states), heads)
    x_heads, raw_heads, bc_heads = (
        lax.all_to_all(x_send, "ctx", split_axis=1, concat_axis=0, tiled=True),
        lax.all_to_all(dt_raw[0], "ctx", split_axis=1, concat_axis=0, tiled=True),
        lax.all_to_all(bc_send, "ctx", split_axis=1, concat_axis=0, tiled=True),
    )
    empty_ids = jnp.full((lag,), -1, jnp.int32)
    taps_x = lax.dynamic_slice_in_dim(
        conv_x[0].reshape(lag + 1, heads, head_dim), first_head, local_heads, 1
    )
    taps_bc = lax.dynamic_slice_in_dim(
        per_head(conv_bc[0].reshape(lag + 1, 2, G, states), heads), first_head, local_heads, 1
    )
    x_conv = causal_taps(
        jnp.zeros((lag,) + x_heads.shape[1:], jnp.bfloat16), x_heads, empty_ids, all_ids, taps_x
    )
    bc_conv = causal_taps(
        jnp.zeros((lag,) + bc_heads.shape[1:], jnp.bfloat16), bc_heads, empty_ids, all_ids, taps_bc
    )
    bias_heads = lax.dynamic_slice_in_dim(dt_bias[0], first_head, local_heads)
    rates = -jnp.exp(lax.dynamic_slice_in_dim(a_log[0], first_head, local_heads))
    skip = lax.dynamic_slice_in_dim(d_skip[0], first_head, local_heads)
    step_size = jax.nn.softplus(raw_heads.astype(jnp.float32) + bias_heads[None, :])
    _, local = state_space(x_conv, bc_conv, step_size, rates, skip, all_ids)
    attention_mixture = local.astype(jnp.bfloat16)
    mixed_tokens = lax.all_to_all(
        attention_mixture, "ctx", split_axis=0, concat_axis=1, tiled=True
    ).reshape(tokens_here, heads * head_dim)
    gated = mixed_tokens.astype(jnp.float32) * jax.nn.silu(z_in[0].astype(jnp.float32))
    grouped = gated.reshape(tokens_here, G, heads * head_dim // G)
    factor = lax.rsqrt(jnp.mean(grouped * grouped, axis=-1, keepdims=True) + norm_eps)
    mamba_out = (
        (grouped * factor).reshape(tokens_here, heads * head_dim) * norm_gain[0][None, :]
    ).astype(jnp.bfloat16)
    ratio = AH // KVH
    queries = query[0].reshape(tokens_here, KVH, ratio, HD)
    query_pos = place * tokens_here + jnp.arange(tokens_here)
    logit_scale = 1.0 / math.sqrt(HD)
    initial = (
        jnp.full((KVH, ratio, tokens_here), -1e30, jnp.float32),
        jnp.zeros((KVH, ratio, tokens_here), jnp.float32),
        jnp.zeros((KVH, ratio, tokens_here, HD), jnp.float32),
    )
    carry = initial
    key_piece = lax.all_gather(keys[0], "ctx", axis=0, tiled=True)
    value_piece = lax.all_gather(values[0], "ctx", axis=0, tiled=True)
    count = key_piece.shape[0]
    width = math.gcd(count, 512)
    key_blocks = key_piece.reshape(count // width, width, KVH, HD)
    value_blocks = value_piece.reshape(count // width, width, KVH, HD)

    def visit(running, item):
        key_block, value_block, order = item
        first = order * width
        key_ids = lax.dynamic_slice_in_dim(all_ids, first, width)
        key_pos = first + jnp.arange(width)
        allowed = (query_pos[:, None] >= key_pos[None, :]) & (own_ids[:, None] == key_ids[None, :])
        largest, totals, accum = running
        attention_logits = (
            jnp.einsum("tgrd,mgd->grtm", queries, key_block, preferred_element_type=jnp.float32)
            * logit_scale
        )
        masked = jnp.where(allowed, attention_logits, -1e30)
        newest = jnp.maximum(largest, jnp.max(masked, axis=-1))
        weight = jnp.where(allowed, jnp.exp(masked - newest[..., None]), 0.0)
        correct = jnp.exp(largest - newest)
        totals = totals * correct + jnp.sum(weight, axis=-1)
        accum = accum * correct[..., None] + jnp.einsum(
            "grtm,mgd->grtd",
            weight.astype(jnp.bfloat16),
            value_block,
            preferred_element_type=jnp.float32,
        )
        running = (newest, totals, accum)
        return (running, None)

    carry, _ = lax.scan(
        visit, carry, (key_blocks, value_blocks, jnp.arange(count // width, dtype=jnp.int32))
    )
    largest, totals, accum = carry
    attended = accum / totals[..., None]
    attended = (
        jnp.transpose(attended, (2, 0, 1, 3)).reshape(tokens_here, AH * HD).astype(jnp.bfloat16)
    )
    handoff = from_behind(attended, "pipe", 1)
    return (mamba_out[None], handoff[None])


def solution(mesh):
    in_specs = (
        P("pipe", "ctx", None),
        P("pipe", "ctx", None),
        P("pipe", "ctx", None),
        P("pipe", "ctx", None),
        P("pipe", None),
        P("pipe", None),
        P("pipe", None),
        P("pipe", None, None),
        P("pipe", None, None),
        P("pipe", None),
        P("pipe", "ctx"),
        P("pipe", "ctx", None),
        P("pipe", "ctx", None),
        P("pipe", "ctx", None),
    )
    out_specs = (P("pipe", "ctx", None), P("pipe", "ctx", None))
    return jax.shard_map(
        on_device, mesh=mesh, in_specs=in_specs, out_specs=out_specs, check_vma=False
    )
```

profile of v0, /device:TPU:0, one launch (start us, length us, event | category | flops | bytes accessed | tf_op | source)
XLA Modules:
  0.0 315.3 jit_solution(9040418585861244815)
XLA Ops:
  0.6 0.8 copy.89
  1.5 0.7 reshape.218
  2.2 6.3 %all-to-all-start = ((bf16[8,2,512]{2,1,0:T(2,128)(2,1)}), bf16[8,2,512]{2,1,0:T(2,128)(2,1)S(1)}, u32[]{:S(2)}, u32[]{:S(2)}) async-start(bf16[8,2,512]{2,1,0:T(2,128)(2,1)} %reshape.218), calls=%async_computation | async-start | bytes 32768 | tf_op jit(solution)/shard_map/all_to_all | solution.py:129
  8.5 4.3 %reshape_squeeze.16 = bf16[64,128,64]{2,1,0:T(8,128)(2,1)} reshape(bf16[1,64,8192]{2,1,0:T(8,128)(2,1)} %param.16) | data formatting | bytes 2097152 | tf_op jit(solution)/shard_map/reshape;squeeze | solution.py:125
  12.7 3.0 copy.144
  15.7 2.7 reshape.220
  18.4 5.1 %all-to-all-start.1 = ((bf16[8,2,32768]{2,1,0:T(2,128)(2,1)}), bf16[8,2,32768]{2,1,0:T(2,128)(2,1)S(1)}, u32[]{:S(2)}, u32[]{:S(2)}) async-start(bf16[8,2,32768]{2,1,0:T(2,128)(2,1)} %reshape.220), calls=%async_computation.1 | async-start | bytes 2097152 | tf_op jit(solution)/shard_map/all_to_all | solution.py:128
  23.7 6.1 %broadcast_in_dim.176 = bf16[64,4,32,2,128]{4,3,0,2,1:T(2,128)(2,1)} broadcast(bf16[64,4,2,128]{3,2,0,1:T(2,128)(2,1)S(1)} %copy.94), dimensions={0,1,3,4} | broadcast | bytes 4325376 | tf_op jit(solution)/shard_map/broadcast_in_dim | solution.py:42
  29.8 7.6 %reshape_reshape.7 = bf16[64,128,256]{2,0,1:T(8,128)(2,1)} reshape(bf16[64,4,32,2,128]{4,3,0,2,1:T(2,128)(2,1)} %broadcast_in_dim.176) | data formatting | bytes 8388608 | tf_op jit(solution)/shard_map/reshape;reshape | solution.py:43
  37.5 12.6 %all-to-all-done.1 = bf16[8,2,32768]{2,1,0:T(2,128)(2,1)S(1)} async-done(((bf16[8,2,32768]{2,1,0:T(2,128)(2,1)}), bf16[8,2,32768]{2,1,0:T(2,128)(2,1)S(1)}, u32[]{:S(2)}, u32[]{:S(2)}) %all-to-all-start.1) | async-done | bytes 1048608 | tf_op jit(solution)/shard_map/all_to_all | solution.py:128
  50.1 4.6 %all-to-all-start.2 = ((bf16[64,128,256]{2,0,1:T(8,128)(2,1)}), bf16[64,128,256]{2,0,1:T(8,128)(2,1)}, u32[]{:S(2)}, u32[]{:S(2)}) async-start(bf16[64,128,256]{2,0,1:T(8,128)(2,1)} %reshape_reshape.7), calls=%async_computation.2 | async-start | bytes 8388608 | tf_op jit(solution)/shard_map/all_to_all | solution.py:130
  55.2 0.6 dynamic-slice.3
  56.6 92.2 %all-reduce.3 = s32[512]{0:T(512)S(1)} all-reduce(s32[512]{0:T(512)S(1)} %bitcast_dynamic-update-slice_fusion), channel_id=2, replica_groups=mesh['pipe'=4,'ctx'=8] {'ctx'}, use_global_device_ids=true, to_apply=%add.3 | all-reduce | flops 512 | bytes 4096 | tf_op jit(solution)/shard_map/all_gather | solution.py:122
  148.8 14.2 %all-gather.1 = bf16[1,512,256]{2,1,0:T(8,128)(2,1)S(1)} all-gather(bf16[1,64,256]{2,1,0:T(8,128)(2,1)S(1)} %copy-done.11), channel_id=3, replica_groups=mesh['pipe'=4,'ctx'=8] {'ctx'}, dimensions={1}, use_global_device_ids=true | all-gather | bytes 294912 | tf_op jit(solution)/shard_map/all_gather | solution.py:170
  163.7 0.6 fusion.63
  164.4 0.6 fusion.55
  165.0 0.7 fusion.56
  165.7 0.7 fusion.47
  166.6 0.8 compare_select_fusion
  167.4 3.1 reshape.221
  170.5 2.9 copy.92
  173.5 3.2 %all_to_all.48 = bf16[512,16,64]{0,2,1:T(8,128)(2,1)S(1)} reshape(bf16[8,64,16,64]{1,0,3,2:T(8,128)(2,1)} %bitcast.252) | data formatting | bytes 2097152 | tf_op jit(solution)/shard_map/all_to_all | solution.py:128
  176.7 2.2 multiply_convert_fusion.2
  179.0 1.2 copy.143
  180.2 4.7 %copy.96 = bf16[8,64,16,256]{3,2,1,0:T(8,128)(2,1)S(1)} copy(bf16[8,64,16,256]{3,1,2,0:T(8,128)(2,1)} %bitcast.17) | data formatting | bytes 8388608 | tf_op jit(solution)/shard_map/all_to_all | solution.py:130
  184.9 7.8 %multiply_convert_fusion = bf16[512,16,256]{2,1,0:T(8,128)(2,1)} fusion(bf16[512,16,256]{2,1,0:T(8,128)(2,1)S(1)} %bitcast.248, f32[16,256]{1,0:T(8,128)S(1)} %get-tuple-element.192, f32[16,256]{1,0:T(8,128)S(1)} %get-tuple-element.190, f32[16,256]{1,0:T(8,128)S(1)} %get-tuple-element.191, f32[16,256]{1,0:T(8,128)S(1)} %get-tuple-element.189, ...), kind=kLoop, calls=%fused_computation.49 | loop fusion | flops 39845888 | bytes 8455680 | tf_op jit(solution)/shard_map/convert_element_type | solution.py:34
  192.7 31.1 %while.3 = (s32[]{:T(128)}, f32[16,64,128]{2,1,0:T(8,128)S(1)}, s32[]{:T(128)}, bf16[2,256,16,64]{1,3,2,0:T(8,128)(2,1)}, s32[2,256]{1,0:T(2,128)S(1)}, /*index=...) while((s32[]{:T(128)}, f32[16,64,128]{2,1,0:T(8,128)S(1)}, ...), condition=%wide.region_3.4_spmd.clone, body=%wide.region_0.3_spmd.clone.sunk | while | flops 882074176 | bytes 19326392 | solution.py:94
  192.7 0.8 constant_dynamic-slice_fusion.11
  193.6 0.6 reduce-window.14
  194.4 1.7 constant_dynamic-slice_fusion.9
  196.1 0.7 copy.155
  197.0 3.6 %fusion.87 = f32[256,16,64]{0,2,1:T(8,128)} fusion(f32[256,16]{0,1:T(8,128)S(1)} %bitcast.258, f32[256,16]{0,1:T(8,128)S(1)} %bitcast_bitcast_fusion.2, pred[256,256]{0,1:T(8,128)(4,1)S(1)} %fusion.86, bf16[256,16,256]{2,0,1:T(8,128)(2,1)S(1)} %bitcast.242, bf16[2,256,16,64]{1,3,2,0:T(8,128)(2,1)} %get-tuple-element.310, s32[]{:T(128)} %get-tuple-element.289), kind=kOutput, calls=%fused_computation.5.clone.1 | convolution fusion | flops 408944640 | bytes 3785216 | tf_op jit(solution)/shard_map/while/body/eval_jaxpr/tsh,shp->thp/dot_general | solution.py:67
  200.8 0.6 dynamic-slice.38
  201.5 0.6 broadcast_compare_fusion.3
  202.2 3.4 %fusion.88 = bf16[2,256,16,64]{1,3,2,0:T(8,128)(2,1)} fusion(bf16[2,256,16,64]{1,3,2,0:T(8,128)(2,1)} %get-tuple-element.292, s32[]{:T(128)} %get-tuple-element.289, f32[256,16,64]{0,2,1:T(8,128)} %fusion.87, bf16[256,16,256]{2,0,1:T(8,128)(2,1)S(1)} %bitcast.243, f32[16]{0:T(128)S(1)} %get-tuple-element.312, f32[256,16]{0,1:T(8,128)S(1)} %get-tuple-element.274, ...), kind=kOutput, calls=%fused_computation.11.clone.1 | convolution fusion | flops 404094976 | bytes 4211713 | tf_op jit(solution)/shard_map/while/body/eval_jaxpr/thn,hpn->thp/dot_general | solution.py:70
  206.2 1.4 convolution_add_fusion.2
  208.3 0.8 constant_dynamic-slice_fusion.11
  209.1 0.6 reduce-window.14
  210.0 1.7 constant_dynamic-slice_fusion.9
  211.7 0.7 copy.155
  212.6 3.6 %fusion.87 = f32[256,16,64]{0,2,1:T(8,128)} fusion(f32[256,16]{0,1:T(8,128)S(1)} %bitcast.258, f32[256,16]{0,1:T(8,128)S(1)} %bitcast_bitcast_fusion.2, pred[256,256]{0,1:T(8,128)(4,1)S(1)} %fusion.86, bf16[256,16,256]{2,0,1:T(8,128)(2,1)S(1)} %bitcast.242, bf16[2,256,16,64]{1,3,2,0:T(8,128)(2,1)} %get-tuple-element.310, s32[]{:T(128)} %get-tuple-element.289), kind=kOutput, calls=%fused_computation.5.clone.1 | convolution fusion | flops 408944640 | bytes 3785216 | tf_op jit(solution)/shard_map/while/body/eval_jaxpr/tsh,shp->thp/dot_general | solution.py:67
  216.4 0.6 dynamic-slice.38
  217.0 0.6 broadcast_compare_fusion.3
  217.8 3.4 %fusion.88 = bf16[2,256,16,64]{1,3,2,0:T(8,128)(2,1)} fusion(bf16[2,256,16,64]{1,3,2,0:T(8,128)(2,1)} %get-tuple-element.292, s32[]{:T(128)} %get-tuple-element.289, f32[256,16,64]{0,2,1:T(8,128)} %fusion.87, bf16[256,16,256]{2,0,1:T(8,128)(2,1)S(1)} %bitcast.243, f32[16]{0:T(128)S(1)} %get-tuple-element.312, f32[256,16]{0,1:T(8,128)S(1)} %get-tuple-element.274, ...), kind=kOutput, calls=%fused_computation.11.clone.1 | convolution fusion | flops 404094976 | bytes 4211713 | tf_op jit(solution)/shard_map/while/body/eval_jaxpr/thn,hpn->thp/dot_general | solution.py:70
  221.8 1.4 convolution_add_fusion.2
  223.8 3.0 copy.115
  226.8 2.7 reshape.222
  229.5 4.6 %all-to-all-start.3 = ((bf16[8,2,32768]{2,1,0:T(2,128)(2,1)}), bf16[8,2,32768]{2,1,0:T(2,128)(2,1)}, u32[]{:S(2)}, u32[]{:S(2)}) async-start(bf16[8,2,32768]{2,1,0:T(2,128)(2,1)} %reshape.222), calls=%async_computation.3 | async-start | bytes 2097152 | tf_op jit(solution)/shard_map/all_to_all | solution.py:151
  234.1 2.7 fusion.31
  236.8 30.7 %all-gather.2 = bf16[1,512,256]{2,1,0:T(8,128)(2,1)S(1)} all-gather(bf16[1,64,256]{2,1,0:T(8,128)(2,1)S(1)} %copy-done.12), channel_id=4, replica_groups=mesh['pipe'=4,'ctx'=8] {'ctx'}, dimensions={1}, use_global_device_ids=true | all-gather | bytes 294912 | tf_op jit(solution)/shard_map/all_gather | solution.py:171
  267.7 3.6 %fusion.32 = f32[4,8,64]{2,1,0:T(8,128)S(1)} fusion(f32[4,512,64,8]{1,2,3,0:T(8,128)} %get-tuple-element.203, f32[4,8,64]{2,1,0:T(8,128)S(1)} %get-tuple-element.198, pred[64,512]{1,0:T(8,128)(4,1)S(1)} %copy-done.3), kind=kLoop, calls=%fused_computation.55 | loop fusion | flops 5240832 | bytes 4243456 | tf_op jit(solution)/shard_map/while/body/eval_jaxpr/reduce_sum | solution.py:192
  271.3 1.5 divide_convert_fusion
  273.5 1.5 collective-permute-start
  275.1 3.2 %reshape.196 = f32[64,8,16,64]{3,2,1,0:T(8,128)} reshape(bf16[1,64,8192]{2,1,0:T(8,128)(2,1)S(1)} %copy-done.2) | data formatting | bytes 3145728 | tf_op jit(solution)/shard_map/convert_element_type | solution.py:154
  278.3 5.5 %copy.105 = f32[64,8,16,64]{0,1,3,2:T(8,128)} copy(f32[64,8,16,64]{3,2,1,0:T(8,128)} %reshape.196) | data formatting | bytes 4194304 | tf_op jit(solution)/shard_map/convert_element_type | solution.py:154
  283.8 3.1 reshape.223
  286.9 2.5 copy.102
  289.4 4.0 %reshape.198 = f32[8,64,16,64]{1,0,3,2:T(8,128)} reshape(bf16[512,16,64]{0,2,1:T(8,128)(2,1)} %copy.102) | data formatting | bytes 3145728 | tf_op jit(solution)/shard_map/convert_element_type | solution.py:154
  293.4 4.9 %multiply_reduce_fusion = f32[64,8]{0,1:T(8,128)S(1)} fusion(f32[64,8,16,64]{0,1,3,2:T(8,128)} %copy.105, f32[8,64,16,64]{1,0,3,2:T(8,128)} %reshape.198), kind=kLoop, calls=%fused_computation.52 | loop fusion | flops 3669504 | bytes 4196352 | tf_op jit(solution)/shard_map/reduce_sum | solution.py:156
  298.8 2.4 mul.292
  301.2 6.3 %copy.103 = f32[64,8,16,64]{3,2,1,0:T(8,128)} copy(f32[64,8,16,64]{0,1,3,2:T(8,128)} %bitcast.246) | data formatting | bytes 4194304 | tf_op jit(solution)/shard_map/convert_element_type | solution.py:154
  307.5 3.5 %reshape.195 = f32[1,64,8192]{2,1,0:T(8,128)S(1)} reshape(f32[64,8,16,64]{3,2,1,0:T(8,128)} %copy.103) | data formatting | bytes 4194304 | tf_op jit(solution)/shard_map/convert_element_type | solution.py:154
  311.1 3.5 %multiply_convert_fusion.1 = bf16[1,64,8192]{2,1,0:T(8,128)(2,1)} fusion(f32[1,64,8192]{2,1,0:T(8,128)} %mul.292, f32[1,64,8192]{2,1,0:T(8,128)S(1)} %reshape.195, f32[8192]{0:T(1024)S(1)} %bitcast.262, bf16[1,64,8192]{2,1,0:T(8,128)(2,1)} %param.17), kind=kLoop, calls=%fused_computation.57 | loop fusion | flops 4718592 | bytes 6324224 | tf_op jit(solution)/shard_map/convert_element_type | solution.py:159
  314.6 0.7 copy.174
  (106 shorter events, 4.8 us)
Async XLA Ops:
  2.2 16.2 %all-to-all-start = ((bf16[8,2,512]{2,1,0:T(2,128)(2,1)}), bf16[8,2,512]{2,1,0:T(2,128)(2,1)S(1)}, u32[]{:S(2)}, u32[]{:S(2)}) async-start(bf16[8,2,512]{2,1,0:T(2,128)(2,1)} %reshape.218), calls=%async_computation | async-start | bytes 32768 | tf_op jit(solution)/shard_map/all_to_all | solution.py:129
  12.7 10.7 %copy-start.5 = (bf16[1,64,1024]{2,1,0:T(8,128)(2,1)S(1)}, bf16[1,64,1024]{2,1,0:T(8,128)(2,1)}, u32[]{:S(2)}) copy-start(bf16[1,64,1024]{2,1,0:T(8,128)(2,1)} %param.18) | copy-start | bytes 393220
  18.4 31.7 %all-to-all-start.1 = ((bf16[8,2,32768]{2,1,0:T(2,128)(2,1)}), bf16[8,2,32768]{2,1,0:T(2,128)(2,1)S(1)}, u32[]{:S(2)}, u32[]{:S(2)}) async-start(bf16[8,2,32768]{2,1,0:T(2,128)(2,1)} %reshape.220), calls=%async_computation.1 | async-start | bytes 2097152 | tf_op jit(solution)/shard_map/all_to_all | solution.py:128
  37.4 17.3 %copy-start.15 = (bf16[1,4,1024]{2,1,0:T(4,128)(2,1)S(1)}, bf16[1,4,1024]{2,1,0:T(4,128)(2,1)}, u32[]{:S(2)}) copy-start(bf16[1,4,1024]{2,1,0:T(4,128)(2,1)} %param.24) | copy-start | bytes 24580
  37.4 17.7 %copy-start.6 = (bf16[1,4,8192]{2,1,0:T(4,128)(2,1)S(1)}, bf16[1,4,8192]{2,1,0:T(4,128)(2,1)}, u32[]{:S(2)}) copy-start(bf16[1,4,8192]{2,1,0:T(4,128)(2,1)} %param.23) | copy-start | bytes 196612
  37.4 17.8 %copy-start.23 = (u32[32]{0:T(128)S(1)}, u32[32]{0:T(128)}, u32[]{:S(2)}) copy-start(u32[32]{0:T(128)} %constant.111) | copy-start | bytes 388
  37.4 19.1 %copy-start.19 = (s32[1,64]{1,0:T(1,128)S(1)}, s32[1,64]{1,0:T(1,128)}, u32[]{:S(2)}) copy-start(s32[1,64]{1,0:T(1,128)} %param.26) | copy-start | bytes 772
  37.4 111.4 %copy-start.11 = (bf16[1,64,256]{2,1,0:T(8,128)(2,1)S(1)}, bf16[1,64,256]{2,1,0:T(8,128)(2,1)}, u32[]{:S(2)}) copy-start(bf16[1,64,256]{2,1,0:T(8,128)(2,1)} %param.28) | copy-start | bytes 98308
  37.4 125.7 %copy-start.4 = (bf16[1,64,2048]{2,1,0:T(8,128)(2,1)S(1)}, bf16[1,64,2048]{2,1,0:T(8,128)(2,1)}, u32[]{:S(2)}) copy-start(bf16[1,64,2048]{2,1,0:T(8,128)(2,1)} %param.27) | copy-start | bytes 786436
  37.4 126.2 %copy-start.22 = (f32[1,128]{1,0:T(1,128)S(1)}, f32[1,128]{1,0:T(1,128)}, u32[]{:S(2)}) copy-start(f32[1,128]{1,0:T(1,128)} %param.20) | copy-start | bytes 1540
  37.5 126.8 %copy-start.20 = (f32[1,128]{1,0:T(1,128)S(1)}, f32[1,128]{1,0:T(1,128)}, u32[]{:S(2)}) copy-start(f32[1,128]{1,0:T(1,128)} %param.21) | copy-start | bytes 1540
  37.5 126.8 %copy-start.21 = (f32[1,128]{1,0:T(1,128)S(1)}, f32[1,128]{1,0:T(1,128)}, u32[]{:S(2)}) copy-start(f32[1,128]{1,0:T(1,128)} %param.22) | copy-start | bytes 1540
  50.1 4.6 %copy-start.1 = (bf16[8,2,32768]{2,1,0:T(2,128)(2,1)}, bf16[8,2,32768]{2,1,0:T(2,128)(2,1)S(1)}, u32[]{:S(2)}) copy-start(bf16[8,2,32768]{2,1,0:T(2,128)(2,1)S(1)} %all-to-all-done.1) | copy-start | bytes 3145732
  50.1 130.1 %all-to-all-start.2 = ((bf16[64,128,256]{2,0,1:T(8,128)(2,1)}), bf16[64,128,256]{2,0,1:T(8,128)(2,1)}, u32[]{:S(2)}, u32[]{:S(2)}) async-start(bf16[64,128,256]{2,0,1:T(8,128)(2,1)} %reshape_reshape.7), calls=%async_computation.2 | async-start | bytes 8388608 | tf_op jit(solution)/shard_map/all_to_all | solution.py:130
  170.5 6.2 %copy-start.8 = (f32[16,64]{1,0:T(8,128)S(1)}, f32[16,64]{1,0:T(8,128)}, u32[]{:S(2)}) copy-start(f32[16,64]{1,0:T(8,128)} %get-tuple-element.194) | copy-start | bytes 12292
  170.5 6.2 %copy-start.9 = (f32[16,64]{1,0:T(8,128)S(1)}, f32[16,64]{1,0:T(8,128)}, u32[]{:S(2)}) copy-start(f32[16,64]{1,0:T(8,128)} %get-tuple-element.195) | copy-start | bytes 12292
  170.5 6.2 %copy-start.10 = (f32[16,64]{1,0:T(8,128)S(1)}, f32[16,64]{1,0:T(8,128)}, u32[]{:S(2)}) copy-start(f32[16,64]{1,0:T(8,128)} %get-tuple-element.196) | copy-start | bytes 12292
  170.5 6.2 %copy-start.16 = (pred[512]{0:T(512)(128)(4,1)S(1)}, pred[512]{0:T(512)(128)(4,1)}, u32[]{:S(2)}) copy-start(pred[512]{0:T(512)(128)(4,1)} %get-tuple-element.199) | copy-start | bytes 1540
  170.5 6.2 %copy-start.17 = (pred[512]{0:T(512)(128)(4,1)S(1)}, pred[512]{0:T(512)(128)(4,1)}, u32[]{:S(2)}) copy-start(pred[512]{0:T(512)(128)(4,1)} %get-tuple-element.200) | copy-start | bytes 1540
  170.5 6.2 %copy-start.18 = (pred[512]{0:T(512)(128)(4,1)S(1)}, pred[512]{0:T(512)(128)(4,1)}, u32[]{:S(2)}) copy-start(pred[512]{0:T(512)(128)(4,1)} %get-tuple-element.201) | copy-start | bytes 1540
  184.9 7.8 %copy-start.13 = (f32[16]{0:T(128)S(1)}, f32[16]{0:T(128)}, u32[]{:S(2)}) copy-start(f32[16]{0:T(128)} %fusion.63) | copy-start | bytes 196
  200.6 7.0 %copy-start.14 = (f32[16]{0:T(128)S(1)}, f32[16]{0:T(128)}, u32[]{:S(2)}) copy-start(f32[16]{0:T(128)} %get-tuple-element.345) | copy-start | bytes 196 | tf_op jit(solution)/shard_map/while
  216.2 7.0 %copy-start.14 = (f32[16]{0:T(128)S(1)}, f32[16]{0:T(128)}, u32[]{:S(2)}) copy-start(f32[16]{0:T(128)} %get-tuple-element.345) | copy-start | bytes 196 | tf_op jit(solution)/shard_map/while
  223.8 10.3 %copy-start.3 = (pred[64,512]{1,0:T(8,128)(4,1)S(1)}, pred[64,512]{1,0:T(8,128)(4,1)}, u32[]{:S(2)}) copy-start(pred[64,512]{1,0:T(8,128)(4,1)} %fusion.47) | copy-start | bytes 98308
  229.5 7.3 %copy-start.12 = (bf16[1,64,256]{2,1,0:T(8,128)(2,1)S(1)}, bf16[1,64,256]{2,1,0:T(8,128)(2,1)}, u32[]{:S(2)}) copy-start(bf16[1,64,256]{2,1,0:T(8,128)(2,1)} %param.29) | copy-start | bytes 98308
  229.5 54.3 %all-to-all-start.3 = ((bf16[8,2,32768]{2,1,0:T(2,128)(2,1)}), bf16[8,2,32768]{2,1,0:T(2,128)(2,1)}, u32[]{:S(2)}, u32[]{:S(2)}) async-start(bf16[8,2,32768]{2,1,0:T(2,128)(2,1)} %reshape.222), calls=%async_computation.3 | async-start | bytes 2097152 | tf_op jit(solution)/shard_map/all_to_all | solution.py:151
  267.6 3.6 %copy-start = (f32[4,512,64,8]{1,2,3,0:T(8,128)S(1)}, f32[4,512,64,8]{1,2,3,0:T(8,128)}, u32[]{:S(2)}) copy-start(f32[4,512,64,8]{1,2,3,0:T(8,128)} %get-tuple-element.203) | copy-start | bytes 12582916
  271.3 3.8 %copy-start.2 = (bf16[1,64,8192]{2,1,0:T(8,128)(2,1)S(1)}, bf16[1,64,8192]{2,1,0:T(8,128)(2,1)}, u32[]{:S(2)}) copy-start(bf16[1,64,8192]{2,1,0:T(8,128)(2,1)} %param.17) | copy-start | bytes 3145732
  273.5 10.3 %collective-permute-start = (bf16[64,2048]{1,0:T(8,128)(2,1)S(1)}, bf16[64,2048]{1,0:T(8,128)(2,1)S(1)}, u32[]{:S(2)}, u32[]{:S(2)}) collective-permute-start(bf16[64,2048]{1,0:T(8,128)(2,1)S(1)} %convert_element_type.151), channel_id=1, source_target_pairs={{0,8},{8,16},{16,24},{24,0},{1,9},{9,17},{17,25},{25,1},{2,10},{10... | collective-permute-start | bytes 786440 | tf_op jit(solution)/shard_map/ppermute | solution.py:17
  307.5 3.5 %copy-start.7 = (f32[1,8192]{1,0:T(1,128)S(1)}, f32[1,8192]{1,0:T(1,128)}, u32[]{:S(2)}) copy-start(f32[1,8192]{1,0:T(1,128)} %param.25) | copy-start | bytes 98308
where the time goes:
time: 317 us; the launch traced here: 315 us
  blocking collectives  137 us (43%)
  local copies, waits for them, and re-layouts  89.4 us (28%)
  other arithmetic  28.6 us (9%)
  starting transfers between devices  22.1 us (7%)
  matrix products  21.1 us (7%)
  waiting for transfers between devices  12.6 us (4%)
    all_gather x1, blocking collectives, on_device(): all_ids = lax.all_gather(own_ids, 'ctx', axis=0, tiled=True)  92.2 us
    all_gather x1, blocking collectives, on_device(): value_piece = lax.all_gather(values[0], 'ctx', axis=0, tiled=True)  30.7 us
    unnamed x57, local copies, waits for them, and re-layouts  14.6 us
    all_gather x1, blocking collectives, on_device(): key_piece = lax.all_gather(keys[0], 'ctx', axis=0, tiled=True)  14.2 us
    convert_element_type x3, local copies, waits for them, and re-layouts, on_device(): mixed_tokens.astype(jnp.float32) * jax.nn.silu(z_in[0].astype(jnp.float32))  13.9 us
    all_to_all x1, waiting for transfers between devices, on_device(): lax.all_to_all(x_send, 'ctx', split_axis=1, concat_axis=0, tiled=True)  12.6 us
    convert_element_type x2, other arithmetic, causal_taps(): return jax.nn.silu(summed).astype(jnp.bfloat16)  10 us
    convert_element_type x2, local copies, waits for them, and re-layouts, on_device(): z_in[0].astype(jnp.float32)  8.7 us
  transfers between devices with their start and end apart: 5, of which 1 were waited for; matrix products, arithmetic and copies ran while one was open for 18% of the time, Pallas kernels for 0%

commit v1 on v0

--- a/solution.py
+++ b/solution.py
@@ -9,6 +9,29 @@
 KVH = 4
 HD = 64
 norm_eps = 1e-05
+
+
+def in_blocks(x, dim, size):
+    dims = x.shape
+    pieces = x.reshape(*dims[:dim], size, dims[dim] // size, *dims[dim + 1 :])
+    return jnp.moveaxis(pieces, dim, 0)
+
+
+def joined_along(tiles, dim):
+    shape = list(tiles.shape[1:])
+    shape[dim] *= tiles.shape[0]
+    return jnp.moveaxis(tiles, 0, dim).reshape(shape)
+
+
+def rotated_exchange(array, axis, split_dim, concat_dim):
+    count, index = (lax.axis_size(axis), lax.axis_index(axis))
+    pieces = in_blocks(array, split_dim, count)
+    outs = [pieces[index]]
+    for turn in range(1, count):
+        sent = pieces[(index + turn) % count]
+        outs.append(lax.ppermute(sent, axis, [(i, (i + turn) % count) for i in range(count)]))
+    pieces = jnp.stack(outs)[(index - jnp.arange(count)) % count]
+    return joined_along(pieces, concat_dim)
 
 
 def from_behind(value, axis, steps):
@@ -127,7 +150,7 @@
     x_heads, raw_heads, bc_heads = (
         lax.all_to_all(x_send, "ctx", split_axis=1, concat_axis=0, tiled=True),
         lax.all_to_all(dt_raw[0], "ctx", split_axis=1, concat_axis=0, tiled=True),
-        lax.all_to_all(bc_send, "ctx", split_axis=1, concat_axis=0, tiled=True),
+        rotated_exchange(bc_send, "ctx", 1, 0),
     )
     empty_ids = jnp.full((lag,), -1, jnp.int32)
     taps_x = lax.dynamic_slice_in_dim(

time: 317 us -> 305 us (0.962)
  blocking collectives: 137 us -> 103 us
  starting transfers between devices: 22.1 us -> 32.5 us
  waiting for transfers between devices: 12.6 us -> 18.7 us
    all_gather x1, blocking collectives: 92.2 us -> 54.7 us  [on_device(): all_ids = lax.all_gather(own_ids, 'ctx', axis=0, tiled=True)]
    ppermute x0 -> x7, waiting for transfers between devices: none -> 18.7 us  [rotated_exchange(): lax.ppermute(sent, axis, [(i, (i + turn) % count) for i in range(count)])]
    all_to_all x1, waiting for transfers between devices: 12.6 us -> 0.01 us  [on_device(): lax.all_to_all(x_send, 'ctx', split_axis=1, concat_axis=0, tiled=True)]
    ppermute x0 -> x7, starting transfers between devices: none -> 12.1 us  [rotated_exchange(): lax.ppermute(sent, axis, [(i, (i + turn) % count) for i in range(count)])]
    unnamed x57 -> x72, local copies, waits for them, and re-layouts: 14.6 us -> 24.1 us
    another operation x2 -> x1, local copies, waits for them, and re-layouts: 7.75 us -> 0.17 us  [per_head(): return spread.reshape(leading + (heads, 2 * states))]
    broadcast_in_dim x2 -> x3, local copies, waits for them, and re-layouts: 6.28 us -> 0.45 us  [per_head(): spread = jnp.repeat(moved, heads // groups, axis=-3)]
    all_to_all x1, starting transfers between devices: 4.59 us -> 10 us  [on_device(): lax.all_to_all(attention_mixture, 'ctx', split_axis=0, concat_axis=1, til...]
  transfers between devices with their start and end apart: 5 -> 11, of which waited for: 1 -> 2; matrix products, arithmetic and copies ran while one was open for 18% -> 22% of each run, Pallas kernels for 0% -> 0%
where the time goes in v1:
time: 305 us; the launch traced here: 304 us
  blocking collectives  103 us (34%)
  local copies, waits for them, and re-layouts  91.6 us (30%)
  starting transfers between devices  32.5 us (11%)
  other arithmetic  31.4 us (10%)
  matrix products  22.1 us (7%)
  waiting for transfers between devices  18.7 us (6%)
    all_gather x1, blocking collectives, on_device(): all_ids = lax.all_gather(own_ids, 'ctx', axis=0, tiled=True)  54.7 us
    all_gather x1, blocking collectives, on_device(): value_piece = lax.all_gather(values[0], 'ctx', axis=0, tiled=True)  29.7 us
    unnamed x72, local copies, waits for them, and re-layouts  24.1 us
    ppermute x7, waiting for transfers between devices, rotated_exchange(): lax.ppermute(sent, axis, [(i, (i + turn) % count) for i in range(count)])  18.7 us
    all_gather x1, blocking collectives, on_device(): key_piece = lax.all_gather(keys[0], 'ctx', axis=0, tiled=True)  18.3 us
    convert_element_type x2, other arithmetic, causal_taps(): return jax.nn.silu(summed).astype(jnp.bfloat16)  12.3 us
    convert_element_type x3, local copies, waits for them, and re-layouts, on_device(): mixed_tokens.astype(jnp.float32) * jax.nn.silu(z_in[0].astype(jnp.float32))  12.2 us
    ppermute x7, starting transfers between devices, rotated_exchange(): lax.ppermute(sent, axis, [(i, (i + turn) % count) for i in range(count)])  12.1 us
  transfers between devices with their start and end apart: 11, of which 2 were waited for; matrix products, arithmetic and copies ran while one was open for 22% of the time, Pallas kernels for 0%

profile of v1, /device:TPU:0, one launch (start us, length us, event | category | flops | bytes accessed | tf_op | source)
XLA Modules:
  0.0 303.9 jit_solution(1617159550529535011)
XLA Ops:
  0.8 1.1 reshape_squeeze.18
  2.5 0.8 squeeze.80
  3.8 0.9 squeeze.81
  4.7 2.6 collective-permute-start.1
  7.3 0.8 squeeze.82
  8.1 2.6 collective-permute-start.2
  10.7 0.9 squeeze.83
  11.6 1.2 collective-permute-start.3
  12.8 0.8 squeeze.84
  13.6 1.1 collective-permute-start.4
  15.6 4.0 %all-to-all-start = ((bf16[8,2,512]{2,1,0:T(2,128)(2,1)}), bf16[8,2,512]{2,1,0:T(2,128)(2,1)}, u32[]{:S(2)}, u32[]{:S(2)}) async-start(bf16[8,2,512]{2,1,0:T(2,128)(2,1)} %reshape.327), calls=%async_computation | async-start | bytes 32768 | tf_op jit(solution)/shard_map/all_to_all | solution.py:152
  19.6 0.9 broadcast_dynamic-update-slice_fusion
  22.7 54.7 %all-reduce.3 = s32[512]{0:T(512)S(1)} all-reduce(s32[512]{0:T(512)S(1)} %bitcast_dynamic-update-slice_fusion.7), channel_id=2, replica_groups=mesh['pipe'=4,'ctx'=8] {'ctx'}, use_global_device_ids=true, to_apply=%add.3 | all-reduce | flops 512 | bytes 4096 | tf_op jit(solution)/shard_map/all_gather | solution.py:145
  79.5 18.3 %all-gather.1 = bf16[1,512,256]{2,1,0:T(8,128)(2,1)S(1)} all-gather(bf16[1,64,256]{2,1,0:T(8,128)(2,1)S(1)} %copy-done.13), channel_id=3, replica_groups=mesh['pipe'=4,'ctx'=8] {'ctx'}, dimensions={1}, use_global_device_ids=true | all-gather | bytes 294912 | tf_op jit(solution)/shard_map/all_gather | solution.py:193
  99.8 3.2 %reshape_squeeze.16 = bf16[64,128,64]{2,1,0:T(8,128)(2,1)} reshape(bf16[1,64,8192]{2,1,0:T(8,128)(2,1)S(1)} %copy-done.3) | data formatting | bytes 2097152 | tf_op jit(solution)/shard_map/reshape;squeeze | solution.py:148
  103.0 3.0 copy.138
  106.0 2.7 reshape.329
  108.9 1.3 reshape_squeeze.19
  110.2 5.0 %all-to-all-start.1 = ((bf16[8,2,32768]{2,1,0:T(2,128)(2,1)}), bf16[8,2,32768]{2,1,0:T(2,128)(2,1)}, u32[]{:S(2)}, u32[]{:S(2)}) async-start(bf16[8,2,32768]{2,1,0:T(2,128)(2,1)} %reshape.329), calls=%async_computation.1 | async-start | bytes 2097152 | tf_op jit(solution)/shard_map/all_to_all | solution.py:151
  117.0 3.9 %collective-permute-start.5 = (bf16[64,16,256]{2,1,0:T(8,128)(2,1)S(1)}, bf16[64,16,256]{2,1,0:T(8,128)(2,1)S(1)}, u32[]{:S(2)}, u32[]{:S(2)}) collective-permute-start(bf16[64,16,256]{2,1,0:T(8,128)(2,1)S(1)} %squeeze.85), channel_id=1, source_target_pairs={{0,6},{1,7},{2,0},{3,1},{4,2},{5,3},{6,4},{7,5},{8,14},{9,15},{10,... | collective-permute-start | bytes 1572872 | tf_op jit(solution)/shard_map/ppermute | solution.py:32
  120.8 1.9 bitcast_dynamic-update-slice_fusion.6
  123.0 1.9 bitcast_dynamic-update-slice_fusion.5
  124.9 1.9 bitcast_dynamic-update-slice_fusion.4
  126.8 1.9 bitcast_dynamic-update-slice_fusion.3
  128.7 1.9 bitcast_dynamic-update-slice_fusion.2
  130.5 15.9 %collective-permute-done.5 = bf16[64,16,256]{2,1,0:T(8,128)(2,1)S(1)} collective-permute-done((bf16[64,16,256]{2,1,0:T(8,128)(2,1)S(1)}, bf16[64,16,256]{2,1,0:T(8,128)(2,1)S(1)}, u32[]{:S(2)}, u32[]{:S(2)}) %collective-permute-start.5) | collective-permute-done | bytes 524320 | tf_op jit(solution)/shard_map/ppermute | solution.py:32
  146.5 0.8 bitcast_dynamic-update-slice_fusion.1
  147.3 2.7 collective-permute-done.6
  150.0 0.8 bitcast_dynamic-update-slice_fusion
  150.9 5.1 %gather_fusion = bf16[8,64,16,256]{3,2,1,0:T(8,128)(2,1)} fusion(bf16[8,64,16,256]{3,2,1,0:T(8,128)(2,1)} %bitcast_dynamic-update-slice_fusion, s32[1024]{0:T(1024)} %pad_clamp_fusion), kind=kCustom, calls=%fused_computation | custom fusion | bytes 8388640 | tf_op jit(solution)/shard_map/gather | solution.py:33
  156.0 10.1 %multiply_convert_fusion = bf16[512,16,256]{2,1,0:T(8,128)(2,1)} fusion(bf16[512,16,256]{2,1,0:T(8,128)(2,1)} %bitcast.277, f32[16,256]{1,0:T(8,128)S(1)} %copy-done.5, f32[16,256]{1,0:T(8,128)S(1)} %get-tuple-element.190, f32[16,256]{1,0:T(8,128)S(1)} %get-tuple-element.191, f32[16,256]{1,0:T(8,128)S(1)} %get-tuple-element.189, ...), kind=kLoop, calls=%fused_computation.50 | loop fusion | flops 39845888 | bytes 8455680 | tf_op jit(solution)/shard_map/convert_element_type | solution.py:57
  166.1 3.1 %reshape.330 = bf16[128,64,64]{2,1,0:T(8,128)(2,1)S(1)} reshape(bf16[8,2,32768]{2,1,0:T(2,128)(2,1)} %all-to-all-done.1) | data formatting | bytes 2097152
  169.2 2.8 copy.89
  172.1 3.2 %all_to_all.35 = bf16[512,16,64]{0,2,1:T(8,128)(2,1)S(1)} reshape(bf16[8,64,16,64]{1,0,3,2:T(8,128)(2,1)} %bitcast.281) | data formatting | bytes 2097152 | tf_op jit(solution)/shard_map/all_to_all | solution.py:151
  175.3 2.2 multiply_convert_fusion.2
  177.5 1.1 copy.137
  178.7 30.1 %while.3 = (s32[]{:T(128)}, f32[16,64,128]{2,1,0:T(8,128)S(1)}, s32[]{:T(128)}, bf16[2,256,16,64]{1,3,2,0:T(8,128)(2,1)}, s32[2,256]{1,0:T(2,128)S(1)}, /*index=...) while((s32[]{:T(128)}, f32[16,64,128]{2,1,0:T(8,128)S(1)}, ...), condition=%wide.region_3.4_spmd.clone, body=%wide.region_0.3_spmd.clone.sunk | while | flops 882074176 | bytes 19326100 | solution.py:117
  179.7 1.7 constant_dynamic-slice_fusion.13
  182.2 3.7 %fusion.93 = f32[256,16,64]{0,2,1:T(8,128)} fusion(f32[256,16]{0,1:T(8,128)S(1)} %bitcast.287, f32[256,16]{0,1:T(8,128)S(1)} %bitcast_bitcast_fusion.2, pred[256,256]{0,1:T(8,128)(4,1)S(1)} %fusion.92, bf16[256,16,256]{2,0,1:T(8,128)(2,1)S(1)} %bitcast.271, bf16[2,256,16,64]{1,3,2,0:T(8,128)(2,1)} %get-tuple-element.318, s32[]{:T(128)} %get-tuple-element.297), kind=kOutput, calls=%fused_computation.6.clone.1 | convolution fusion | flops 408944640 | bytes 3785216 | tf_op jit(solution)/shard_map/while/body/eval_jaxpr/tsh,shp->thp/dot_general | solution.py:90
  187.5 3.4 %fusion.94 = bf16[2,256,16,64]{1,3,2,0:T(8,128)(2,1)} fusion(bf16[2,256,16,64]{1,3,2,0:T(8,128)(2,1)} %get-tuple-element.300, s32[]{:T(128)} %get-tuple-element.297, f32[256,16,64]{0,2,1:T(8,128)} %fusion.93, bf16[256,16,256]{2,0,1:T(8,128)(2,1)S(1)} %bitcast.272, f32[16]{0:T(128)S(1)} %get-tuple-element.320, f32[256,16]{0,1:T(8,128)S(1)} %get-tuple-element.282, ...), kind=kOutput, calls=%fused_computation.12.clone.1 | convolution fusion | flops 404094976 | bytes 4211713 | tf_op jit(solution)/shard_map/while/body/eval_jaxpr/thn,hpn->thp/dot_general | solution.py:93
  191.6 1.4 convolution_add_fusion.2
  194.7 1.7 constant_dynamic-slice_fusion.13
  197.3 3.7 %fusion.93 = f32[256,16,64]{0,2,1:T(8,128)} fusion(f32[256,16]{0,1:T(8,128)S(1)} %bitcast.287, f32[256,16]{0,1:T(8,128)S(1)} %bitcast_bitcast_fusion.2, pred[256,256]{0,1:T(8,128)(4,1)S(1)} %fusion.92, bf16[256,16,256]{2,0,1:T(8,128)(2,1)S(1)} %bitcast.271, bf16[2,256,16,64]{1,3,2,0:T(8,128)(2,1)} %get-tuple-element.318, s32[]{:T(128)} %get-tuple-element.297), kind=kOutput, calls=%fused_computation.6.clone.1 | convolution fusion | flops 408944640 | bytes 3785216 | tf_op jit(solution)/shard_map/while/body/eval_jaxpr/tsh,shp->thp/dot_general | solution.py:90
  202.6 3.4 %fusion.94 = bf16[2,256,16,64]{1,3,2,0:T(8,128)(2,1)} fusion(bf16[2,256,16,64]{1,3,2,0:T(8,128)(2,1)} %get-tuple-element.300, s32[]{:T(128)} %get-tuple-element.297, f32[256,16,64]{0,2,1:T(8,128)} %fusion.93, bf16[256,16,256]{2,0,1:T(8,128)(2,1)S(1)} %bitcast.272, f32[16]{0:T(128)S(1)} %get-tuple-element.320, f32[256,16]{0,1:T(8,128)S(1)} %get-tuple-element.282, ...), kind=kOutput, calls=%fused_computation.12.clone.1 | convolution fusion | flops 404094976 | bytes 4211713 | tf_op jit(solution)/shard_map/while/body/eval_jaxpr/thn,hpn->thp/dot_general | solution.py:93
  206.7 1.4 convolution_add_fusion.2
  208.8 3.0 copy.109
  211.8 2.7 reshape.331
  214.4 10.0 %all-to-all-start.2 = ((bf16[8,2,32768]{2,1,0:T(2,128)(2,1)}), bf16[8,2,32768]{2,1,0:T(2,128)(2,1)S(1)}, u32[]{:S(2)}, u32[]{:S(2)}) async-start(bf16[8,2,32768]{2,1,0:T(2,128)(2,1)} %reshape.331), calls=%async_computation.2 | async-start | bytes 2097152 | tf_op jit(solution)/shard_map/all_to_all | solution.py:174
  224.5 3.8 %fusion.31 = (f32[4,8,64]{2,1,0:T(8,128)S(1)}, f32[4,512,64,8]{1,2,3,0:T(8,128)}) fusion(pred[64,512]{1,0:T(8,128)(4,1)S(1)} %fusion.47, bf16[512,4,64,1]{0,2,3,1:T(8,128)(2,1)S(1)} %bitcast.283, bf16[64,4,8,64]{3,2,1,0:T(8,128)(2,1)} %reshape_squeeze.19), kind=kOutput, calls=%fused_computation.55 | convolution fusion | flops 137361408 | bytes 4759552 | tf_op jit(solution)/shard_map/while/body/eval_jaxpr/tgrd,mgd->grtm/dot_general | solution.py:208
  228.2 29.7 %all-gather.2 = bf16[1,512,256]{2,1,0:T(8,128)(2,1)S(1)} all-gather(bf16[1,64,256]{2,1,0:T(8,128)(2,1)S(1)} %copy-done.14), channel_id=4, replica_groups=mesh['pipe'=4,'ctx'=8] {'ctx'}, dimensions={1}, use_global_device_ids=true | all-gather | bytes 294912 | tf_op jit(solution)/shard_map/all_gather | solution.py:194
  258.1 3.6 %fusion.32 = f32[4,8,64]{2,1,0:T(8,128)S(1)} fusion(f32[4,512,64,8]{1,2,3,0:T(8,128)} %get-tuple-element.211, f32[4,8,64]{2,1,0:T(8,128)S(1)} %get-tuple-element.206, pred[64,512]{1,0:T(8,128)(4,1)S(1)} %fusion.47), kind=kLoop, calls=%fused_computation.56 | loop fusion | flops 5240832 | bytes 4243456 | tf_op jit(solution)/shard_map/while/body/eval_jaxpr/reduce_sum | solution.py:215
  261.7 1.5 divide_convert_fusion
  264.0 1.5 collective-permute-start.7
  265.5 3.3 %reshape.297 = f32[64,8,16,64]{3,2,1,0:T(8,128)} reshape(bf16[1,64,8192]{2,1,0:T(8,128)(2,1)S(1)} %copy-done.1) | data formatting | bytes 3145728 | tf_op jit(solution)/shard_map/convert_element_type | solution.py:177
  268.7 5.5 %copy.100 = f32[64,8,16,64]{0,1,3,2:T(8,128)} copy(f32[64,8,16,64]{3,2,1,0:T(8,128)} %reshape.297) | data formatting | bytes 4194304 | tf_op jit(solution)/shard_map/convert_element_type | solution.py:177
  274.2 1.4 reshape.332
  275.7 1.7 copy.97
  277.3 2.4 reshape.299
  279.8 6.3 %copy.98 = f32[64,8,16,64]{3,2,1,0:T(8,128)} copy(f32[64,8,16,64]{0,1,3,2:T(8,128)} %bitcast.275) | data formatting | bytes 4194304 | tf_op jit(solution)/shard_map/convert_element_type | solution.py:177
  286.0 3.5 %reshape.296 = f32[1,64,8192]{2,1,0:T(8,128)S(1)} reshape(f32[64,8,16,64]{3,2,1,0:T(8,128)} %copy.98) | data formatting | bytes 4194304 | tf_op jit(solution)/shard_map/convert_element_type | solution.py:177
  289.6 4.9 %multiply_reduce_fusion = f32[64,8]{0,1:T(8,128)S(1)} fusion(f32[64,8,16,64]{0,1,3,2:T(8,128)} %copy.100, f32[8,64,16,64]{1,0,3,2:T(8,128)} %reshape.299), kind=kLoop, calls=%fused_computation.53 | loop fusion | flops 3669504 | bytes 4196352 | tf_op jit(solution)/shard_map/reduce_sum | solution.py:179
  294.6 1.7 mul.291
  296.3 3.7 %mul.292 = f32[1,64,8192]{2,1,0:T(8,128)} reshape(f32[64,4,2048]{2,1,0:T(4,128)} %mul.291) | data formatting | bytes 4194304 | tf_op jit(solution)/shard_map/mul | solution.py:181
  300.0 3.2 %multiply_convert_fusion.1 = bf16[1,64,8192]{2,1,0:T(8,128)(2,1)} fusion(f32[1,64,8192]{2,1,0:T(8,128)} %mul.292, f32[1,64,8192]{2,1,0:T(8,128)S(1)} %reshape.296, f32[8192]{0:T(1024)S(1)} %bitcast.291, bf16[1,64,8192]{2,1,0:T(8,128)(2,1)S(1)} %copy-done.2), kind=kLoop, calls=%fused_computation.58 | loop fusion | flops 4718592 | bytes 6324224 | tf_op jit(solution)/shard_map/convert_element_type | solution.py:182
  (140 shorter events, 18.3 us)
Async XLA Ops:
  0.6 20.7 %copy-start.26 = (u32[32]{0:T(128)S(1)}, u32[32]{0:T(128)}, u32[]{:S(2)}) copy-start(u32[32]{0:T(128)} %constant.170) | copy-start | bytes 388
  0.6 14.1 %copy-start.16 = (bf16[1,64,128]{2,1,0:T(8,128)(2,1)S(1)}, bf16[1,64,128]{2,1,0:T(8,128)(2,1)}, u32[]{:S(2)}) copy-start(bf16[1,64,128]{2,1,0:T(8,128)(2,1)} %param.19) | copy-start | bytes 49156
  0.7 20.4 %copy-start.18 = (bf16[1,4,1024]{2,1,0:T(4,128)(2,1)S(1)}, bf16[1,4,1024]{2,1,0:T(4,128)(2,1)}, u32[]{:S(2)}) copy-start(bf16[1,4,1024]{2,1,0:T(4,128)(2,1)} %param.24) | copy-start | bytes 24580
  0.7 22.0 %copy-start.22 = (s32[1,64]{1,0:T(1,128)S(1)}, s32[1,64]{1,0:T(1,128)}, u32[]{:S(2)}) copy-start(s32[1,64]{1,0:T(1,128)} %param.26) | copy-start | bytes 772
  0.7 77.4 %copy-start.6 = (bf16[1,4,8192]{2,1,0:T(4,128)(2,1)S(1)}, bf16[1,4,8192]{2,1,0:T(4,128)(2,1)}, u32[]{:S(2)}) copy-start(bf16[1,4,8192]{2,1,0:T(4,128)(2,1)} %param.23) | copy-start | bytes 196612
  0.7 78.8 %copy-start.13 = (bf16[1,64,256]{2,1,0:T(8,128)(2,1)S(1)}, bf16[1,64,256]{2,1,0:T(8,128)(2,1)}, u32[]{:S(2)}) copy-start(bf16[1,64,256]{2,1,0:T(8,128)(2,1)} %param.28) | copy-start | bytes 98308
  0.7 97.1 %copy-start.23 = (f32[1,128]{1,0:T(1,128)S(1)}, f32[1,128]{1,0:T(1,128)}, u32[]{:S(2)}) copy-start(f32[1,128]{1,0:T(1,128)} %param.21) | copy-start | bytes 1540
  0.7 97.1 %copy-start.24 = (f32[1,128]{1,0:T(1,128)S(1)}, f32[1,128]{1,0:T(1,128)}, u32[]{:S(2)}) copy-start(f32[1,128]{1,0:T(1,128)} %param.22) | copy-start | bytes 1540
  0.7 97.8 %copy-start.25 = (f32[1,128]{1,0:T(1,128)S(1)}, f32[1,128]{1,0:T(1,128)}, u32[]{:S(2)}) copy-start(f32[1,128]{1,0:T(1,128)} %param.20) | copy-start | bytes 1540
  0.7 99.1 %copy-start.3 = (bf16[1,64,8192]{2,1,0:T(8,128)(2,1)S(1)}, bf16[1,64,8192]{2,1,0:T(8,128)(2,1)}, u32[]{:S(2)}) copy-start(bf16[1,64,8192]{2,1,0:T(8,128)(2,1)} %param.16) | copy-start | bytes 3145732
  3.3 113.6 %collective-permute-start = (bf16[64,16,256]{2,1,0:T(8,128)(2,1)}, bf16[64,16,256]{2,1,0:T(8,128)(2,1)}, u32[]{:S(2)}, u32[]{:S(2)}) collective-permute-start(bf16[64,16,256]{2,1,0:T(8,128)(2,1)} %squeeze.80), channel_id=1, source_target_pairs={{0,1},{1,2},{2,3},{3,4},{4,5},{5,6},{6,7},{7,0},{8,9},{9,10},{10,1... | collective-permute-start | bytes 1572872 | tf_op jit(solution)/shard_map/ppermute | solution.py:32
  4.7 118.0 %collective-permute-start.1 = (bf16[64,16,256]{2,1,0:T(8,128)(2,1)}, bf16[64,16,256]{2,1,0:T(8,128)(2,1)}, u32[]{:S(2)}, u32[]{:S(2)}) collective-permute-start(bf16[64,16,256]{2,1,0:T(8,128)(2,1)} %squeeze.81), channel_id=1, source_target_pairs={{0,2},{1,3},{2,4},{3,5},{4,6},{5,7},{6,0},{7,1},{8,10},{9,11},{10,... | collective-permute-start | bytes 1572872 | tf_op jit(solution)/shard_map/ppermute | solution.py:32
  8.1 116.8 %collective-permute-start.2 = (bf16[64,16,256]{2,1,0:T(8,128)(2,1)}, bf16[64,16,256]{2,1,0:T(8,128)(2,1)}, u32[]{:S(2)}, u32[]{:S(2)}) collective-permute-start(bf16[64,16,256]{2,1,0:T(8,128)(2,1)} %squeeze.82), channel_id=1, source_target_pairs={{0,3},{1,4},{2,5},{3,6},{4,7},{5,0},{6,1},{7,2},{8,11},{9,12},{10,... | collective-permute-start | bytes 1572872 | tf_op jit(solution)/shard_map/ppermute | solution.py:32
  11.6 115.2 %collective-permute-start.3 = (bf16[64,16,256]{2,1,0:T(8,128)(2,1)}, bf16[64,16,256]{2,1,0:T(8,128)(2,1)}, u32[]{:S(2)}, u32[]{:S(2)}) collective-permute-start(bf16[64,16,256]{2,1,0:T(8,128)(2,1)} %squeeze.83), channel_id=1, source_target_pairs={{0,4},{1,5},{2,6},{3,7},{4,0},{5,1},{6,2},{7,3},{8,12},{9,13},{10,... | collective-permute-start | bytes 1572872 | tf_op jit(solution)/shard_map/ppermute | solution.py:32
  13.6 115.1 %collective-permute-start.4 = (bf16[64,16,256]{2,1,0:T(8,128)(2,1)}, bf16[64,16,256]{2,1,0:T(8,128)(2,1)}, u32[]{:S(2)}, u32[]{:S(2)}) collective-permute-start(bf16[64,16,256]{2,1,0:T(8,128)(2,1)} %squeeze.84), channel_id=1, source_target_pairs={{0,5},{1,6},{2,7},{3,0},{4,1},{5,2},{6,3},{7,4},{8,13},{9,14},{10,... | collective-permute-start | bytes 1572872 | tf_op jit(solution)/shard_map/ppermute | solution.py:32
  15.6 94.6 %all-to-all-start = ((bf16[8,2,512]{2,1,0:T(2,128)(2,1)}), bf16[8,2,512]{2,1,0:T(2,128)(2,1)}, u32[]{:S(2)}, u32[]{:S(2)}) async-start(bf16[8,2,512]{2,1,0:T(2,128)(2,1)} %reshape.327), calls=%async_computation | async-start | bytes 32768 | tf_op jit(solution)/shard_map/all_to_all | solution.py:152
  103.0 5.8 %copy-start.4 = (bf16[1,64,2048]{2,1,0:T(8,128)(2,1)S(1)}, bf16[1,64,2048]{2,1,0:T(8,128)(2,1)}, u32[]{:S(2)}) copy-start(bf16[1,64,2048]{2,1,0:T(8,128)(2,1)} %param.27) | copy-start | bytes 786436
  110.2 55.9 %all-to-all-start.1 = ((bf16[8,2,32768]{2,1,0:T(2,128)(2,1)}), bf16[8,2,32768]{2,1,0:T(2,128)(2,1)}, u32[]{:S(2)}, u32[]{:S(2)}) async-start(bf16[8,2,32768]{2,1,0:T(2,128)(2,1)} %reshape.329), calls=%async_computation.1 | async-start | bytes 2097152 | tf_op jit(solution)/shard_map/all_to_all | solution.py:151
  117.0 29.5 %collective-permute-start.5 = (bf16[64,16,256]{2,1,0:T(8,128)(2,1)S(1)}, bf16[64,16,256]{2,1,0:T(8,128)(2,1)S(1)}, u32[]{:S(2)}, u32[]{:S(2)}) collective-permute-start(bf16[64,16,256]{2,1,0:T(8,128)(2,1)S(1)} %squeeze.85), channel_id=1, source_target_pairs={{0,6},{1,7},{2,0},{3,1},{4,2},{5,3},{6,4},{7,5},{8,14},{9,15},{10,... | collective-permute-start | bytes 1572872 | tf_op jit(solution)/shard_map/ppermute | solution.py:32
  122.8 27.2 %collective-permute-start.6 = (bf16[64,16,256]{2,1,0:T(8,128)(2,1)S(1)}, bf16[64,16,256]{2,1,0:T(8,128)(2,1)S(1)}, u32[]{:S(2)}, u32[]{:S(2)}) collective-permute-start(bf16[64,16,256]{2,1,0:T(8,128)(2,1)S(1)} %squeeze.86), channel_id=1, source_target_pairs={{0,7},{1,0},{2,1},{3,2},{4,3},{5,4},{6,5},{7,6},{8,15},{9,8},{10,9... | collective-permute-start | bytes 1572872 | tf_op jit(solution)/shard_map/ppermute | solution.py:32
  150.8 5.1 %copy-start.5 = (f32[16,256]{1,0:T(8,128)S(1)}, f32[16,256]{1,0:T(8,128)}, u32[]{:S(2)}) copy-start(f32[16,256]{1,0:T(8,128)} %get-tuple-element.192) | copy-start | bytes 49156
  150.8 5.2 %copy-start.19 = (pred[512]{0:T(512)(128)(4,1)S(1)}, pred[512]{0:T(512)(128)(4,1)}, u32[]{:S(2)}) copy-start(pred[512]{0:T(512)(128)(4,1)} %get-tuple-element.207) | copy-start | bytes 1540
  150.8 5.2 %copy-start.20 = (pred[512]{0:T(512)(128)(4,1)S(1)}, pred[512]{0:T(512)(128)(4,1)}, u32[]{:S(2)}) copy-start(pred[512]{0:T(512)(128)(4,1)} %get-tuple-element.208) | copy-start | bytes 1540
  150.8 5.2 %copy-start.21 = (pred[512]{0:T(512)(128)(4,1)S(1)}, pred[512]{0:T(512)(128)(4,1)}, u32[]{:S(2)}) copy-start(pred[512]{0:T(512)(128)(4,1)} %get-tuple-element.209) | copy-start | bytes 1540
  169.2 6.1 %copy-start.9 = (f32[16,64]{1,0:T(8,128)S(1)}, f32[16,64]{1,0:T(8,128)}, u32[]{:S(2)}) copy-start(f32[16,64]{1,0:T(8,128)} %get-tuple-element.201) | copy-start | bytes 12292
  169.2 6.1 %copy-start.10 = (f32[16,64]{1,0:T(8,128)S(1)}, f32[16,64]{1,0:T(8,128)}, u32[]{:S(2)}) copy-start(f32[16,64]{1,0:T(8,128)} %get-tuple-element.202) | copy-start | bytes 12292
  169.2 6.1 %copy-start.11 = (f32[16,64]{1,0:T(8,128)S(1)}, f32[16,64]{1,0:T(8,128)}, u32[]{:S(2)}) copy-start(f32[16,64]{1,0:T(8,128)} %get-tuple-element.203) | copy-start | bytes 12292
  169.2 6.1 %copy-start.12 = (f32[16,64]{1,0:T(8,128)S(1)}, f32[16,64]{1,0:T(8,128)}, u32[]{:S(2)}) copy-start(f32[16,64]{1,0:T(8,128)} %get-tuple-element.204) | copy-start | bytes 12292
  172.1 6.6 %copy-start.7 = (s32[2,256]{1,0:T(2,128)S(1)}, s32[2,256]{1,0:T(2,128)}, u32[]{:S(2)}) copy-start(s32[2,256]{1,0:T(2,128)} %reshape.275) | copy-start | bytes 6148
  172.1 6.6 %copy-start.15 = (f32[16]{0:T(128)S(1)}, f32[16]{0:T(128)}, u32[]{:S(2)}) copy-start(f32[16]{0:T(128)} %get-tuple-element.292) | copy-start | bytes 196
  172.1 6.6 %copy-start.17 = (f32[16]{0:T(128)S(1)}, f32[16]{0:T(128)}, u32[]{:S(2)}) copy-start(f32[16]{0:T(128)} %fusion.69) | copy-start | bytes 196
  214.4 13.8 %copy-start.14 = (bf16[1,64,256]{2,1,0:T(8,128)(2,1)S(1)}, bf16[1,64,256]{2,1,0:T(8,128)(2,1)}, u32[]{:S(2)}) copy-start(bf16[1,64,256]{2,1,0:T(8,128)(2,1)} %param.29) | copy-start | bytes 98308
  214.4 59.8 %all-to-all-start.2 = ((bf16[8,2,32768]{2,1,0:T(2,128)(2,1)}), bf16[8,2,32768]{2,1,0:T(2,128)(2,1)S(1)}, u32[]{:S(2)}, u32[]{:S(2)}) async-start(bf16[8,2,32768]{2,1,0:T(2,128)(2,1)} %reshape.331), calls=%async_computation.2 | async-start | bytes 2097152 | tf_op jit(solution)/shard_map/all_to_all | solution.py:174
  258.1 3.6 %copy-start = (f32[4,512,64,8]{1,2,3,0:T(8,128)S(1)}, f32[4,512,64,8]{1,2,3,0:T(8,128)}, u32[]{:S(2)}) copy-start(f32[4,512,64,8]{1,2,3,0:T(8,128)} %get-tuple-element.211) | copy-start | bytes 12582916
  261.7 3.7 %copy-start.1 = (bf16[1,64,8192]{2,1,0:T(8,128)(2,1)S(1)}, bf16[1,64,8192]{2,1,0:T(8,128)(2,1)}, u32[]{:S(2)}) copy-start(bf16[1,64,8192]{2,1,0:T(8,128)(2,1)} %param.17) | copy-start | bytes 3145732
  264.0 10.2 %collective-permute-start.7 = (bf16[64,2048]{1,0:T(8,128)(2,1)S(1)}, bf16[64,2048]{1,0:T(8,128)(2,1)S(1)}, u32[]{:S(2)}, u32[]{:S(2)}) collective-permute-start(bf16[64,2048]{1,0:T(8,128)(2,1)S(1)} %convert_element_type.151), channel_id=1, source_target_pairs={{0,8},{8,16},{16,24},{24,0},{1,9},{9,17},{17,25},{25,1},{2,10},{10... | collective-permute-start | bytes 786440 | tf_op jit(solution)/shard_map/ppermute | solution.py:40
  294.5 5.5 %copy-start.2 = (bf16[1,64,8192]{2,1,0:T(8,128)(2,1)S(1)}, bf16[1,64,8192]{2,1,0:T(8,128)(2,1)}, u32[]{:S(2)}) copy-start(bf16[1,64,8192]{2,1,0:T(8,128)(2,1)} %param.17) | copy-start | bytes 3145732
  294.5 5.5 %copy-start.8 = (f32[1,8192]{1,0:T(1,128)S(1)}, f32[1,8192]{1,0:T(1,128)}, u32[]{:S(2)}) copy-start(f32[1,8192]{1,0:T(1,128)} %param.25) | copy-start | bytes 98308
